TPU v7x, 32 devices: a whole 2x2x4 slice. The times are simulated.
32 devices in a mesh: qrow: 8 (over z, core), kcol: 4 (over y, x).
Axes of the slice: x: 2, y: 2, z: 4, core: 2. Of those that a mesh axis runs over, the one named last changes fastest.
Arguments:
- query_rows: bfloat16 [4096, 512], P(('qrow', 'kcol')), may hold values from -6 to 6
- key_rows: bfloat16 [4096, 512], P(('kcol', 'qrow')), may hold values from -6 to 6
- value_rows: bfloat16 [4096, 512], P(('kcol', 'qrow')), may hold values from -6 to 6
- layer_out: bfloat16 [4096, 512], P(('qrow', 'kcol')), may hold values from -6 to 6
- grad_out: bfloat16 [4096, 512], P(('qrow', 'kcol')), may hold values from -6 to 6
- block_order: int32 [32], replicated, may hold values from 0 to 31, each once
- tile_mask: int32 [32, 32], replicated, may hold values from 0 to 1, as said below
Outputs:
- grad_query: float32 [4096, 512], P(('qrow', 'kcol'))
- grad_key: float32 [4096, 512], P(('kcol', 'qrow'))
- grad_value: float32 [4096, 512], P(('kcol', 'qrow'))
Inputs may be any that keep to these rules, and one draw needn't show every extreme that they name: block_order is a permutation of 0 to 31. tile_mask[a, b] is 1 exactly where logical blocks a and b lie in the same document and b <= a, where documents are runs of consecutive logical blocks; the diagonal is 1.
All inputs are finite; a program needn't handle non-finite values.
Results may differ from a plain program's by a relative error of at most 0.0035.
Values may be sent and summed in bfloat16 or wider, within the bound.
A program may use at most 192 MiB of HBM per device.

v0:
```python
import math

import jax
import jax.numpy as jnp
from jax import lax
from jax.sharding import PartitionSpec as P

HD = 128
H = 4


def merged(x, axis, combine):
    everything = jax.tree.map(lambda part: lax.all_gather(part, axis), x)
    leading = jax.tree.map(lambda part: part[0], everything)

    def step(k, so_far):
        return combine(so_far, jax.tree.map(lambda part: part[k], everything))

    return lax.fori_loop(1, lax.axis_size(axis), step, leading)


def combine_stats(first, second):
    largest = jnp.maximum(first[0], second[0])
    return (
        largest,
        first[1] * jnp.exp(first[0] - largest) + second[1] * jnp.exp(second[0] - largest),
    )


def head_slice(matrix, head_number):
    return matrix[:, head_number * HD : (head_number + 1) * HD]


def tile_grads(query_part, grad_part, delta_part, log_part, allow_part, key_part, value_part):
    score_scale = 1.0 / math.sqrt(HD)
    query_list = []
    key_list = []
    value_list = []
    for head_number in range(H):
        query_head = head_slice(query_part, head_number)
        grad_head = head_slice(grad_part, head_number)
        key_head = head_slice(key_part, head_number)
        value_head = head_slice(value_part, head_number)
        scores = jnp.dot(query_head, key_head.T, preferred_element_type=jnp.float32) * score_scale
        scores = jnp.where(allow_part, scores, -1e30)
        probs = jnp.exp(scores - log_part[head_number][:, None])
        probs_low = probs.astype(jnp.bfloat16)
        dprobs = jnp.dot(grad_head, value_head.T, preferred_element_type=jnp.float32)
        column_delta = delta_part[:, head_number].astype(jnp.float32)[:, None]
        dscores = (probs * (dprobs - column_delta)).astype(jnp.bfloat16)
        query_list.append(
            jnp.dot(dscores, key_head, preferred_element_type=jnp.float32) * score_scale
        )
        key_list.append(
            jnp.dot(dscores.T, query_head, preferred_element_type=jnp.float32) * score_scale
        )
        value_list.append(jnp.dot(probs_low.T, grad_head, preferred_element_type=jnp.float32))
    return (
        jnp.concatenate(query_list, 1),
        jnp.concatenate(key_list, 1),
        jnp.concatenate(value_list, 1),
    )


def body(query_rows, key_rows, value_rows, layer_out, grad_out, block_order, tile_mask):
    score_scale = 1.0 / math.sqrt(HD)
    block_rows = query_rows.shape[0]
    n_qrow = lax.axis_size("qrow")
    n_kcol = lax.axis_size("kcol")
    products = (grad_out.astype(jnp.float32) * layer_out.astype(jnp.float32)).reshape(
        block_rows, H, HD
    )
    delta = jnp.sum(products, axis=2).astype(jnp.bfloat16)
    query_all, grad_all, delta_all = (
        lax.all_gather(query_rows, "kcol", axis=0, tiled=True),
        lax.all_gather(grad_out, "kcol", axis=0, tiled=True),
        lax.all_gather(delta, "kcol", axis=0, tiled=True),
    )
    key_all, value_all = (
        lax.all_gather(key_rows, "qrow", axis=0, tiled=True),
        lax.all_gather(value_rows, "qrow", axis=0, tiled=True),
    )
    query_ids = lax.dynamic_slice_in_dim(block_order, lax.axis_index("qrow") * n_kcol, n_kcol)
    key_ids = lax.dynamic_slice_in_dim(block_order, lax.axis_index("kcol") * n_qrow, n_qrow)
    row_groups = query_ids.shape[0]
    column_groups = key_ids.shape[0]
    labels = jnp.arange(block_order.shape[0], dtype=jnp.int32)
    pick_query = (query_ids[:, None] == labels[None, :]).astype(jnp.float32)
    pick_key = (key_ids[:, None] == labels[None, :]).astype(jnp.float32)
    tiles = jnp.dot(pick_query, tile_mask.astype(jnp.float32), precision=lax.Precision.HIGHEST)
    tiles = jnp.dot(tiles, pick_key.T, precision=lax.Precision.HIGHEST)
    query_count = row_groups * block_rows
    key_count = column_groups * block_rows
    tile_full = jnp.broadcast_to(
        tiles[:, None, :, None], (row_groups, block_rows, column_groups, block_rows)
    ).reshape(query_count, key_count)
    offsets = jnp.arange(block_rows, dtype=jnp.int32)
    query_pos = (query_ids[:, None] * block_rows + offsets[None, :]).reshape(query_count)
    key_pos = (key_ids[:, None] * block_rows + offsets[None, :]).reshape(key_count)
    allowed = (tile_full > 0.5) & (key_pos[None, :] <= query_pos[:, None])
    maxima_list = []
    totals_list = []
    for head_number in range(H):
        scores = (
            jnp.dot(
                head_slice(query_all, head_number),
                head_slice(key_all, head_number).T,
                preferred_element_type=jnp.float32,
            )
            * score_scale
        )
        scores = jnp.where(allowed, scores, -1e30)
        largest = jnp.max(scores, axis=1)
        maxima_list.append(largest)
        totals_list.append(jnp.sum(jnp.exp(scores - largest[:, None]), axis=1))
    maxima, totals = merged((jnp.stack(maxima_list), jnp.stack(totals_list)), "kcol", combine_stats)
    log_totals = maxima + jnp.log(totals)
    query_terms, key_terms, value_terms = tile_grads(
        query_all, grad_all, delta_all, log_totals, allowed, key_all, value_all
    )
    grad_query = lax.psum_scatter(query_terms, "kcol", scatter_dimension=0, tiled=True)
    grad_key, grad_value = (
        lax.psum_scatter(key_terms, "qrow", scatter_dimension=0, tiled=True),
        lax.psum_scatter(value_terms, "qrow", scatter_dimension=0, tiled=True),
    )
    return (grad_query, grad_key, grad_value)


def solution(mesh):
    placed = (
        P(("qrow", "kcol"), None),
        P(("kcol", "qrow"), None),
        P(("kcol", "qrow"), None),
        P(("qrow", "kcol"), None),
        P(("qrow", "kcol"), None),
        P(),
        P(),
    )
    return jax.shard_map(
        body,
        mesh=mesh,
        in_specs=placed,
        out_specs=(P(("qrow", "kcol"), None), P(("kcol", "qrow"), None), P(("kcol", "qrow"), None)),
        check_vma=False,
    )
```

profile of v0, /device:TPU:0, one launch (start us, length us, event | category | flops | bytes accessed | tf_op | source)
XLA Modules:
  0.0 189.3 jit_solution(184508239583405845)
XLA Ops:
  7.2 0.0 all-gather.7.cloned.1.call-start
  7.2 0.7 all-gather.7.cloned.1.call-update
  7.9 0.0 all-gather.9.cloned.1.call-start
  8.0 0.7 all-gather.9.cloned.1.call-update
  8.7 0.0 reduce-scatter.4.cloned.1.call-start
  8.7 0.7 broadcast_multiply_fusion.1
  9.5 0.7 broadcast_multiply_fusion
  10.2 0.1 add_bitcast_fusion.1
  10.3 0.1 add_bitcast_fusion
  10.3 11.8 %all_gather.33 = bf16[512,512]{1,0:T(8,128)(2,1)S(1)} all-gather(bf16[128,512]{1,0:T(8,128)(2,1)} %param.13), channel_id=1, replica_groups=mesh['qrow'=8,'kcol'=4] {'kcol'}, dimensions={0}, use_global_device_ids=true | all-gather | bytes 655360 | tf_op jit(solution)/shard_map/all_gather | solution.py:76
  22.2 1.2 convert_multiply_fusion
  23.4 0.1 reshape.55
  23.5 0.2 reduce_sum.49
  23.7 8.1 %all_gather.35 = bf16[512,4]{1,0:T(8,128)(2,1)S(1)} all-gather(bf16[128,4]{1,0:T(8,128)(2,1)S(1)} %reduce_sum.49), channel_id=1, replica_groups=mesh['qrow'=8,'kcol'=4] {'kcol'}, dimensions={0}, use_global_device_ids=true | all-gather | bytes 5120 | tf_op jit(solution)/shard_map/all_gather | solution.py:77
  31.8 0.3 convert_reduce_fusion.3
  32.1 9.4 %all_gather.27 = bf16[512,512]{1,0:T(8,128)(2,1)S(1)} all-gather(bf16[128,512]{1,0:T(8,128)(2,1)S(1)} %copy-done.20), channel_id=1, replica_groups=mesh['qrow'=8,'kcol'=4] {'kcol'}, dimensions={0}, use_global_device_ids=true | all-gather | bytes 655360 | tf_op jit(solution)/shard_map/all_gather | solution.py:75
  41.6 0.2 fusion.46
  41.8 0.2 convolution_compare_fusion
  41.9 0.2 broadcast_in_dim.12
  42.2 1.8 fusion.51
  44.0 0.5 exponential_reduce_fusion
  44.5 1.5 copy-done.17
  45.9 0.8 fusion.52
  46.7 0.5 exponential_reduce_fusion.1
  47.2 0.8 fusion.53
  48.0 0.5 exponential_reduce_fusion.2
  48.5 0.8 fusion.54
  49.4 1.3 copy-done.4
  50.7 0.5 exponential_reduce_fusion.3
  51.2 7.8 %all-gather.3 = f32[4,4,512]{2,1,0:T(4,128)S(1)} all-gather(f32[1,4,512]{2,1,0:T(4,128)S(1)} %maximum_bitcast_fusion.1), channel_id=3, replica_groups=mesh['qrow'=8,'kcol'=4] {'kcol'}, dimensions={0}, use_global_device_ids=true | all-gather | bytes 40960 | tf_op jit(solution)/shard_map/all_gather | solution.py:13
  59.1 7.5 %all-gather.2 = f32[4,4,512]{2,1,0:T(4,128)S(1)} all-gather(f32[1,4,512]{2,1,0:T(4,128)S(1)} %maximum_bitcast_fusion), channel_id=2, replica_groups=mesh['qrow'=8,'kcol'=4] {'kcol'}, dimensions={0}, use_global_device_ids=true | all-gather | bytes 40960 | tf_op jit(solution)/shard_map/all_gather | solution.py:13
  66.6 0.2 while.17
  66.8 2.4 %multiply_convert_fusion = bf16[512,1024]{1,0:T(8,128)(2,1)S(1)} fusion(f32[512,1024]{1,0:T(8,128)} %copy-done, f32[512]{0:T(512)S(1)} %get-tuple-element.148, f32[512]{0:T(512)S(1)} %bitcast.69, bf16[1024,512]{1,0:T(8,128)(2,1)} %all-gather.9.cloned.1.call-done, bf16[512,512]{1,0:T(8,128)(2,1)S(1)} %all_gather.33), kind=kOutput, calls=%fused_computation.7 | convolution fusion | flops 136314880 | bytes 3543040 | tf_op jit(solution)/shard_map/dot_general | solution.py:48
  69.2 0.5 convolution_multiply_fusion.4
  69.7 0.5 copy-done.7
  70.2 0.5 multiply_convert_fusion.3
  70.8 0.5 convolution_multiply_fusion.7
  71.3 0.6 copy-done.2
  71.9 1.4 multiply_convert_fusion.2
  73.4 0.5 convolution_multiply_fusion.6
  73.9 1.4 multiply_convert_fusion.1
  75.3 1.1 copy-done.11
  76.4 0.5 convolution_multiply_fusion.5
  76.9 1.1 pad_maximum_fusion.2
  78.0 0.2 reduce-scatter.8.cloned.1.call-start
  78.2 2.3 %fusion.6 = f32[1024,128]{0,1:T(8,128)S(1)} fusion(f32[512,1024]{1,0:T(8,128)} %copy-done, f32[512]{0:T(512)S(1)} %bitcast.70, bf16[512,512]{1,0:T(8,128)(2,1)} %copy-done.13), kind=kOutput, calls=%fused_computation.37 | convolution fusion | flops 135266304 | bytes 2754560 | tf_op jit(solution)/shard_map/dot_general | solution.py:57
  80.5 0.5 fusion.12
  81.1 0.5 fusion.8
  81.7 0.5 copy-done.3
  82.1 0.5 fusion.10
  82.7 1.6 pad_maximum_fusion.1
  84.3 0.0 reduce-scatter.6.cloned.1.call-start
  84.4 1.2 copy-done.8
  85.6 1.4 convolution_multiply_fusion
  87.0 1.3 convolution_multiply_fusion.3
  88.3 0.4 convolution_multiply_fusion.1
  88.6 0.4 convolution_multiply_fusion.2
  89.0 1.5 pad_maximum_fusion
  90.5 15.6 %reduce-scatter.4.cloned.1.call-done = f32[128,512]{0,1:T(8,128)} async-done(((f32[512,512]{0,1:T(8,128)}), f32[128,512]{0,1:T(8,128)}) %reduce-scatter.4.cloned.1.call-update) | async-done | bytes 262160 | tf_op jit(solution)/shard_map/reduce_scatter | solution.py:121
  106.1 1.8 copy.16
  107.9 36.3 %reduce-scatter.8.cloned.1.call-done = f32[128,512]{0,1:T(8,128)} async-done(((f32[1024,512]{0,1:T(8,128)}), f32[128,512]{0,1:T(8,128)}) %reduce-scatter.8.cloned.1.call-update) | async-done | bytes 262160 | tf_op jit(solution)/shard_map/reduce_scatter | solution.py:124
  144.2 1.8 copy.18
  146.0 35.0 %reduce-scatter.6.cloned.1.call-done = f32[128,512]{0,1:T(8,128)} async-done(((f32[1024,512]{0,1:T(8,128)}), f32[128,512]{0,1:T(8,128)}) %reduce-scatter.6.cloned.1.call-update) | async-done | bytes 262160 | tf_op jit(solution)/shard_map/reduce_scatter | solution.py:123
  181.0 1.8 copy.17
  (51 shorter events, 0.3 us)
Async XLA Ops:
  7.2 25.0 %copy-start.20 = (bf16[128,512]{1,0:T(8,128)(2,1)S(1)}, bf16[128,512]{1,0:T(8,128)(2,1)}, u32[]{:S(2)}) copy-start(bf16[128,512]{1,0:T(8,128)(2,1)} %param.9) | copy-start | bytes 393220
  7.2 34.4 %copy-start.21 = (s32[32,32]{1,0:T(8,128)S(1)}, s32[32,32]{1,0:T(8,128)}, u32[]{:S(2)}) copy-start(s32[32,32]{1,0:T(8,128)} %param.15) | copy-start | bytes 12292
  7.2 34.8 %all-gather.7.cloned.1.call-start = ((), (), s32[]{:S(2)}) async-start(), calls=%async_computation.3 | async-start | bytes 1179648 | tf_op jit(solution)/shard_map/all_gather | solution.py:80
  7.9 58.9 %all-gather.9.cloned.1.call-start = ((), (), s32[]{:S(2)}) async-start(), calls=%async_computation.4 | async-start | bytes 1179648 | tf_op jit(solution)/shard_map/all_gather | solution.py:81
  8.7 97.5 %reduce-scatter.4.cloned.1.call-start = ((), (), s32[]{:S(2)}) async-start(), calls=%async_computation.5 | async-start | bytes 1310720 | tf_op jit(solution)/shard_map/reduce_scatter | solution.py:121
  22.2 48.0 %copy-start.13 = (bf16[512,512]{1,0:T(8,128)(2,1)}, bf16[512,512]{1,0:T(8,128)(2,1)S(1)}, u32[]{:S(2)}) copy-start(bf16[512,512]{1,0:T(8,128)(2,1)S(1)} %all_gather.33) | copy-start | bytes 1572868
  41.6 7.0 %copy-start.15 = (bf16[512,512]{1,0:T(8,128)(2,1)}, bf16[512,512]{1,0:T(8,128)(2,1)S(1)}, u32[]{:S(2)}) copy-start(bf16[512,512]{1,0:T(8,128)(2,1)S(1)} %all_gather.27) | copy-start | bytes 1572868
  43.9 2.8 %copy-start = (f32[512,1024]{1,0:T(8,128)}, f32[512,1024]{1,0:T(8,128)S(1)}, u32[]{:S(2)}) copy-start(f32[512,1024]{1,0:T(8,128)S(1)} %get-tuple-element.172) | copy-start | bytes 6291460
  43.9 2.0 %copy-start.17 = (bf16[1024,512]{1,0:T(8,128)(2,1)S(1)}, bf16[1024,512]{1,0:T(8,128)(2,1)}, u32[]{:S(2)}) copy-start(bf16[1024,512]{1,0:T(8,128)(2,1)} %all-gather.7.cloned.1.call-done) | copy-start | bytes 3145732
  48.0 1.4 copy-start.1
  49.4 1.3 copy-start.4
  66.8 2.4 %copy-start.18 = (bf16[1024,512]{1,0:T(8,128)(2,1)S(1)}, bf16[1024,512]{1,0:T(8,128)(2,1)}, u32[]{:S(2)}) copy-start(bf16[1024,512]{1,0:T(8,128)(2,1)} %all-gather.7.cloned.1.call-done) | copy-start | bytes 3145732
  66.8 3.4 %copy-start.5 = (f32[512,1024]{1,0:T(8,128)S(1)}, f32[512,1024]{1,0:T(8,128)}, u32[]{:S(2)}) copy-start(f32[512,1024]{1,0:T(8,128)} %copy-done.4) | copy-start | bytes 6291460
  66.8 3.4 %copy-start.19 = (bf16[1024,512]{1,0:T(8,128)(2,1)S(1)}, bf16[1024,512]{1,0:T(8,128)(2,1)}, u32[]{:S(2)}) copy-start(bf16[1024,512]{1,0:T(8,128)(2,1)} %all-gather.9.cloned.1.call-done) | copy-start | bytes 3145732
  69.2 1.0 copy-start.7
  70.2 1.7 copy-start.2
  70.8 2.6 %copy-start.9 = (bf16[512,1024]{1,0:T(8,128)(2,1)}, bf16[512,1024]{1,0:T(8,128)(2,1)S(1)}, u32[]{:S(2)}) copy-start(bf16[512,1024]{1,0:T(8,128)(2,1)S(1)} %multiply_convert_fusion.3) | copy-start | bytes 3145732
  75.3 1.1 copy-start.11
  78.0 66.2 %reduce-scatter.8.cloned.1.call-start = ((), (), s32[]{:S(2)}) async-start(), calls=%async_computation.7 | async-start | bytes 2359296 | tf_op jit(solution)/shard_map/reduce_scatter | solution.py:124
  78.2 2.3 %copy-start.6 = (f32[512,1024]{1,0:T(8,128)S(1)}, f32[512,1024]{1,0:T(8,128)}, u32[]{:S(2)}) copy-start(f32[512,1024]{1,0:T(8,128)} %copy-done.4) | copy-start | bytes 6291460
  78.2 2.3 %copy-start.14 = (bf16[512,512]{1,0:T(8,128)(2,1)S(1)}, bf16[512,512]{1,0:T(8,128)(2,1)}, u32[]{:S(2)}) copy-start(bf16[512,512]{1,0:T(8,128)(2,1)} %copy-done.13) | copy-start | bytes 1572868
  80.5 1.6 copy-start.3
  84.3 1.3 copy-start.8
  84.3 2.7 %copy-start.10 = (bf16[512,1024]{1,0:T(8,128)(2,1)S(1)}, bf16[512,1024]{1,0:T(8,128)(2,1)}, u32[]{:S(2)}) copy-start(bf16[512,1024]{1,0:T(8,128)(2,1)} %copy-done.9) | copy-start | bytes 3145732
  84.3 96.6 %reduce-scatter.6.cloned.1.call-start = ((), (), s32[]{:S(2)}) async-start(), calls=%async_computation.6 | async-start | bytes 2359296 | tf_op jit(solution)/shard_map/reduce_scatter | solution.py:123
  85.6 2.7 %copy-start.12 = (bf16[512,1024]{1,0:T(8,128)(2,1)S(1)}, bf16[512,1024]{1,0:T(8,128)(2,1)}, u32[]{:S(2)}) copy-start(bf16[512,1024]{1,0:T(8,128)(2,1)} %copy-done.11) | copy-start | bytes 3145732
  85.6 2.7 %copy-start.16 = (bf16[512,512]{1,0:T(8,128)(2,1)S(1)}, bf16[512,512]{1,0:T(8,128)(2,1)}, u32[]{:S(2)}) copy-start(bf16[512,512]{1,0:T(8,128)(2,1)} %copy-done.15) | copy-start | bytes 1572868
Sparse Core Ops, SparseCore 0:
  9.6 24.7 all-gather.6
  36.0 21.7 all-gather.8
  78.1 27.9 reduce-scatter.3
  108.4 35.7 reduce-scatter.7
  146.5 34.4 reduce-scatter.5
where the time goes:
time: 190 us; the launch traced here: 189 us
  waiting for transfers between devices  88.3 us (46%)
  blocking collectives  44.7 us (24%)
  matrix products  19.5 us (10%)
  between operations  14.2 us (7%)
  local copies, waits for them, and re-layouts  12.5 us (7%)
  other arithmetic  9.67 us (5%)
    reduce_scatter x1, waiting for transfers between devices, body(): lax.psum_scatter(value_terms, 'qrow', scatter_dimension=0, tiled=True)  36.3 us
    reduce_scatter x1, waiting for transfers between devices, body(): lax.psum_scatter(key_terms, 'qrow', scatter_dimension=0, tiled=True)  35 us
    reduce_scatter x1, waiting for transfers between devices, body(): lax.psum_scatter(query_terms, 'kcol', scatter_dimension=0, tiled=True)  15.6 us
    all_gather x2, blocking collectives, merged(): everything = jax.tree.map(lambda part: lax.all_gather(part, axis), x)  15.3 us
    unnamed x47, local copies, waits for them, and re-layouts  12.1 us
    all_gather x1, blocking collectives, body(): lax.all_gather(grad_out, 'kcol', axis=0, tiled=True)  11.8 us
    all_gather x1, blocking collectives, body(): lax.all_gather(query_rows, 'kcol', axis=0, tiled=True)  9.41 us
    all_gather x1, blocking collectives, body(): lax.all_gather(delta, 'kcol', axis=0, tiled=True)  8.1 us
  transfers between devices with their start and end apart: 5, of which 3 were waited for; matrix products, arithmetic and copies ran while one was open for 13% of the time, Pallas kernels for 0%

commit v1 on v0

v1 whole, which is shorter than its diff:
```python
import functools
import math

import jax
import jax.numpy as jnp
from jax import lax
from jax.experimental import pallas as pl
from jax.experimental.pallas import tpu as pltpu
from jax.sharding import PartitionSpec as P

HD = 128
H = 4
MESH = pl.DeviceIdType.MESH
NT = (((1,), (1,)), ((), ()))
NN = (((1,), (0,)), ((), ()))
TN = (((0,), (0,)), ((), ()))
F32 = jnp.float32
BF16 = jnp.bfloat16
DROWS = 16
ARRIVAL = (0, 1, 3, 2)


def dot(a, b, dims):
    return lax.dot_general(a, b, dims, preferred_element_type=F32)


def kernel(
    n_qrow, n_kcol,
    order_ref, q_ref, k_ref, v_ref, lo_ref, go_ref, mask_ref,
    gq_ref, gk_ref, gv_ref,
    qs, gs, ks, vs, dbuf, p_buf, m_buf, c_buf, gqt,
    st, st_in, sa, ra, sib_out, sib_in, y_out, y_in, zk_out, zk_in, zq_out, zq_in,
    z_send, z_recv, aq_send, aq_recv, ag_send, ag_recv, bk_send, bk_recv, bv_send, bv_recv,
    s_send, s_recv, ga_send, ga_recv, sib_send, sib_recv, y_send, y_recv,
    zk_send, zk_recv, zq_send, zq_recv, own_sem,
):
    blk = q_ref.shape[0]
    n_a = (n_qrow // (2 * H)) * 2
    n_y = n_kcol // 2
    n_b = n_y * 2
    wide = H * blk
    scale = 1.0 / math.sqrt(HD)
    mq, mk = lax.axis_index("qrow"), lax.axis_index("kcol")
    core, z, r = mq % 2, (mq // 2) % H, mq // (2 * H)
    xb, y = mk % 2, mk // 2
    alpha = r * 2 + xb

    def z_of(d):
        return (z + d) % H

    def z_dev(d):
        return (r * (2 * H) + z_of(d) * 2 + core, mk)

    def a_dev(d):
        other = (alpha + d) % n_a
        return ((other // 2) * (2 * H) + z * 2 + core, y * 2 + other % 2)

    def y_dev(d):
        return (mq, ((y + d) % n_y) * 2 + xb)

    sibling = (r * (2 * H) + z * 2 + (core + 1) % 2, mk)

    def q_block(a, d):
        other = (alpha + a) % n_a
        return ((other // 2) * (2 * H) + z_of(d) * 2 + core) * n_kcol + y * 2 + other % 2

    def k_block(b, d):
        there = ((y + b // 2) % n_y) * 2 + xb
        return there * n_qrow + r * (2 * H) + z_of(d) * 2 + (core + b % 2) % 2

    def cols(d):
        return pl.ds(pl.multiple_of(z_of(d) * HD, HD), HD)

    def remote(src, dst, ss, rs, dev):
        return pltpu.make_async_remote_copy(
            src_ref=src, dst_ref=dst, send_sem=ss, recv_sem=rs, device_id=dev, device_id_type=MESH
        )

    barrier = pltpu.get_barrier_semaphore()
    partners = [z_dev(d) for d in range(1, H)]
    partners += [a_dev(d) for d in range(1, n_a)]
    partners += [y_dev(d) for d in range(1, n_y)] + [sibling]
    for dev in partners:
        pl.semaphore_signal(barrier, inc=1, device_id=dev, device_id_type=MESH)

    for h in range(H):
        at = slice(h * HD, (h + 1) * HD)
        prod = go_ref[:, at].astype(F32) * lo_ref[:, at].astype(F32)
        row = jnp.sum(prod.T, axis=0, keepdims=True)
        dbuf[h] = jnp.broadcast_to(row, (DROWS, blk)).astype(BF16)

    labels = lax.broadcasted_iota(jnp.int32, mask_ref.shape, 0)[:, :1]
    count = jnp.sum(mask_ref[...].astype(F32), axis=1, keepdims=True)
    first = labels.astype(F32) + 1.0 - count
    lane = lax.broadcasted_iota(jnp.int32, (1, blk), 1)

    def q_rows(a):
        pos, low = [], []
        for s in range(H):
            lb = order_ref[q_block(a, s)]
            pos.append(lb * blk + lane)
            f = jnp.sum(jnp.where(labels == lb, first, 0.0), axis=0, keepdims=True)
            low.append(jnp.broadcast_to(f, (1, blk)))
        return jnp.concatenate(pos, 1), jnp.concatenate(low, 1).astype(jnp.int32)

    key_iota = lax.broadcasted_iota(jnp.int32, (blk, wide), 0)
    q_pos = [q_rows(a) for a in range(n_a)]

    pl.semaphore_wait(barrier, len(partners))

    def z_pairs(d, e):
        at = cols(d)
        return [
            (q_ref.at[:, at], qs.at[0, e]),
            (k_ref.at[:, at], ks.at[0, e]),
            (go_ref.at[:, at], gs.at[0, e, pl.ds(0, blk)]),
            (dbuf.at[z_of(d)], gs.at[0, e, pl.ds(blk, DROWS)]),
            (v_ref.at[:, at], vs.at[0, e]),
        ]

    def z_copy(d, i):
        e = H - d
        src, dst = z_pairs(d, e)[i]
        return remote(src, dst, z_send.at[e, i], z_recv.at[e, i], z_dev(d))

    for group in ((0, 1), (2, 3, 4)):
        for d in (2, 1, 3):
            for i in group:
                z_copy(d, i).start()
    own = [
        pltpu.make_async_copy(src, dst, own_sem.at[i]) for i, (src, dst) in enumerate(z_pairs(0, 0))
    ]
    for copy in own:
        copy.start()

    def a_copy(buf, ss, rs, d, s):
        e = n_a - d
        return remote(buf.at[0, s], buf.at[e, s], ss.at[e, s], rs.at[e, s], a_dev(d))

    def y_copy(buf, ss, rs, d, s):
        e = 2 * (n_y - d)
        return remote(buf.at[0, s], buf.at[e, s], ss.at[e, s], rs.at[e, s], y_dev(d))

    def sib_copy(buf, ss, rs, d, s):
        e = 2 * d + 1
        return remote(buf.at[2 * d, s], buf.at[e, s], ss.at[e, s], rs.at[e, s], sibling)

    q_set, g_set = (qs, aq_send, aq_recv), (gs, ag_send, ag_recv)
    k_set, v_set = (ks, bk_send, bk_recv), (vs, bv_send, bv_recv)

    def forward(s, a_set, b_set, group):
        for i in group:
            if s == 0:
                own[i].wait()
            else:
                z_copy(H - s, i).wait_recv()
        for d in range(1, n_y):
            y_copy(*b_set, d, s).start()
        for d in range(1, n_a):
            a_copy(*a_set, d, s).start()
        sib_copy(*b_set, 0, s).start()

    def onward(b_set):
        for d in range(1, n_y):
            for s in ARRIVAL:
                y_copy(*b_set, n_y - d, s).wait_recv()
                sib_copy(*b_set, d, s).start()

    def wait_keys(b_set, b):
        if b % 2:
            for s in range(H):
                sib_copy(*b_set, b // 2, s).wait_recv()

    def wait_queries(a_set, a):
        if a:
            for s in range(H):
                a_copy(*a_set, n_a - a, s).wait_recv()

    def tile_scores(b, a):
        pos, low = q_pos[a]
        qa = qs[a].reshape(wide, HD)
        scores = dot(ks[b].reshape(wide, HD), qa, NT)
        for s in range(H):
            lb = order_ref[k_block(b, s)]
            limit = jnp.where(lb >= low, pos - lb * blk, -1)
            sc = jnp.where(key_iota <= limit, scores[s * blk : (s + 1) * blk] * scale, -1e30)
            m = jnp.max(sc, axis=0, keepdims=True)
            p = jnp.exp(sc - m)
            p_buf[a, b, s] = p
            m_buf[a, b, s] = m
            c_buf[a, b, s] = jnp.sum(p, axis=0, keepdims=True)

    for s in ARRIVAL:
        forward(s, q_set, k_set, (0, 1))
    forward(0, g_set, v_set, (2, 3, 4))
    later = [functools.partial(forward, s, g_set, v_set, (2, 3, 4)) for s in ARRIVAL[1:]]
    tile_scores(0, 0)
    onward(k_set)
    order = [(1, 0)] + [(b, a) for a in range(1, n_a) for b in (0, 1)]
    order += [(b, a) for b in range(2, n_b) for a in range(n_a)]
    ready_a, ready_b = {0}, {0}
    for b, a in order:
        if a not in ready_a:
            wait_queries(q_set, a)
            ready_a.add(a)
        if b not in ready_b:
            wait_keys(k_set, b)
            ready_b.add(b)
        tile_scores(b, a)
        if later:
            later.pop(0)()
    for rest in later:
        rest()

    for a in range(n_a):
        m_all = m_buf[a].reshape(n_b * H, wide)
        m = jnp.max(m_all, axis=0, keepdims=True)
        ls = c_buf[a].reshape(n_b * H, wide) * jnp.exp(m_all - m)
        st[a, 0:1] = m
        st[a, 1:2] = jnp.sum(ls, axis=0, keepdims=True)
        st[a, 2:8] = jnp.zeros((6, wide), F32)

    def s_copy(d):
        e = n_a - d
        return remote(st, st_in.at[e], s_send.at[e], s_recv.at[e], a_dev(d))

    for d in range(1, n_a):
        s_copy(d).start()
    onward(v_set)
    for a in range(1, n_a):
        wait_queries(g_set, a)
    for b in range(1, n_b):
        wait_keys(v_set, b)
    for d in range(1, n_a):
        s_copy(d).wait_recv()
    for a in range(n_a):
        m, l = st[a, 0:1], st[a, 1:2]
        for d in range(1, n_a):
            m2, l2 = st_in[d, (a - d) % n_a, 0:1], st_in[d, (a - d) % n_a, 1:2]
            top = jnp.maximum(m, m2)
            l = l * jnp.exp(m - top) + l2 * jnp.exp(m2 - top)
            m = top
        log_total = m + jnp.log(l)
        c_buf[a] = jnp.exp(m_buf[a] - log_total)

    def sib_sum(d, s):
        return remote(sib_out.at[d, s], sib_in.at[d, s], sib_send.at[d, s], sib_recv.at[d, s], sibling)

    def y_sum(d, s):
        e = n_y - d
        return remote(y_out.at[d, s], y_in.at[e, s], y_send.at[e, s], y_recv.at[e, s], y_dev(d))

    def zk_copy(d):
        e = H - d
        return remote(zk_out.at[d], zk_in.at[e], zk_send.at[e], zk_recv.at[e], z_dev(d))

    def zq_copy(d):
        e = H - d
        return remote(zq_out.at[d], zq_in.at[e], zq_send.at[e], zq_recv.at[e], z_dev(d))

    def ga_copy(d):
        e = n_a - d
        return remote(sa.at[d], ra.at[e], ga_send.at[e], ga_recv.at[e], a_dev(d))

    part = {}

    def compute(s, is_first):
        gk = gv = None
        for a in range(n_a):
            qa = qs[a].reshape(wide, HD)
            ga = gs[a, :, :blk, :].reshape(wide, HD)
            delta = jnp.concatenate([gs[a, t, blk : blk + DROWS, :][0:1].astype(F32) for t in range(H)], 1)
            dp = dot(vs[:, s].reshape(n_b * blk, HD), ga, NT)
            pr = (p_buf[a, :, s] * c_buf[a, :, s]).reshape(n_b * blk, wide)
            ds = (pr * (dp - delta)).astype(BF16)
            dk = dot(ds, qa, NN)
            dv = dot(pr.astype(BF16), ga, NN)
            gk = dk if a == 0 else gk + dk
            gv = dv if a == 0 else gv + dv
            term = dot(ks[:, s].reshape(n_b * blk, HD), ds, TN)
            gqt[a] = term if is_first else gqt[a] + term
        gk = gk * scale
        for d in range(n_y):
            mine = slice(2 * d * blk, (2 * d + 1) * blk)
            other = slice((2 * d + 1) * blk, (2 * d + 2) * blk)
            sib_out[d, s, 0] = gk[other].astype(BF16)
            sib_out[d, s, 1] = gv[other].astype(BF16)
            sib_sum(d, s).start()
            part[d, s] = [gk[mine], gv[mine]]

    def finish_y(s):
        for d in [*range(1, n_y), 0]:
            sib_sum(d, s).wait_recv()
            for i in range(2):
                part[d, s][i] = part[d, s][i] + sib_in[d, s, i].astype(F32)
            if d:
                for i in range(2):
                    y_out[d, s, i] = part[d, s][i].astype(BF16)
                y_sum(d, s).start()

    def finish_z(s):
        total = part[0, s]
        for d in range(1, n_y):
            y_sum(n_y - d, s).wait_recv()
            for i in range(2):
                total[i] = total[i] + y_in[d, s, i].astype(F32)
        if s:
            zk_out[s, 0] = total[0].astype(BF16)
            zk_out[s, 1] = total[1].astype(BF16)
            zk_copy(s).start()
        else:
            gk_ref[:, cols(0)] = total[0]
            gv_ref[:, cols(0)] = total[1]

    turns = (2, 1, 3, 0)
    for i, s in enumerate(turns):
        compute(s, i == 0)
        if i >= 1:
            finish_y(turns[i - 1])
        if i >= 2:
            finish_z(turns[i - 2])
    for a in range(1, n_a):
        sa[a] = (gqt[a].T * scale).astype(BF16).reshape(H, blk, HD)
        ga_copy(a).start()
    finish_y(turns[3])
    finish_z(turns[2])
    total_q = (gqt[0].T * scale).reshape(H, blk, HD)
    for d in range(1, n_a):
        ga_copy(n_a - d).wait_recv()
        total_q = total_q + ra[d].astype(F32)
    for d in (2, 1, 3):
        zq_out[d] = total_q[d].astype(BF16)
        zq_copy(d).start()
    gq_ref[:, cols(0)] = total_q[0]
    finish_z(turns[3])

    for d in (1, 3, 2):
        zk_copy(H - d).wait_recv()
        gk_ref[:, cols(d)] = zk_in[d, 0].astype(F32)
        gv_ref[:, cols(d)] = zk_in[d, 1].astype(F32)
    for d in (1, 3, 2):
        zq_copy(H - d).wait_recv()
        gq_ref[:, cols(d)] = zq_in[d].astype(F32)

    for d in range(1, H):
        for i in range(5):
            z_copy(d, i).wait_send()
        zk_copy(d).wait_send()
        zq_copy(d).wait_send()
    for d in range(1, n_a):
        for s in range(H):
            a_copy(*q_set, d, s).wait_send()
            a_copy(*g_set, d, s).wait_send()
        s_copy(d).wait_send()
        ga_copy(d).wait_send()
    for d in range(n_y):
        for s in range(H):
            sib_copy(*k_set, d, s).wait_send()
            sib_copy(*v_set, d, s).wait_send()
            sib_sum(d, s).wait_send()
            if d:
                y_copy(*k_set, d, s).wait_send()
                y_copy(*v_set, d, s).wait_send()
                y_sum(d, s).wait_send()


def body(n_qrow, n_kcol, query_rows, key_rows, value_rows, layer_out, grad_out, block_order, tile_mask):
    blk = query_rows.shape[0]
    n_a = (n_qrow // (2 * H)) * 2
    n_y = n_kcol // 2
    n_b = n_y * 2
    wide = H * blk
    vm = pl.BlockSpec(memory_space=pltpu.VMEM)
    sm = pl.BlockSpec(memory_space=pltpu.SMEM)
    dma = pltpu.SemaphoreType.DMA
    out = jax.ShapeDtypeStruct(query_rows.shape, F32)
    return pl.pallas_call(
        functools.partial(kernel, n_qrow, n_kcol),
        out_shape=(out, out, out),
        in_specs=[sm, vm, vm, vm, vm, vm, vm],
        out_specs=(vm, vm, vm),
        scratch_shapes=[
            pltpu.VMEM((n_a, H, blk, HD), BF16),
            pltpu.VMEM((n_a, H, blk + DROWS, HD), BF16),
            pltpu.VMEM((n_b, H, blk, HD), BF16),
            pltpu.VMEM((n_b, H, blk, HD), BF16),
            pltpu.VMEM((H, DROWS, blk), BF16),
            pltpu.VMEM((n_a, n_b, H, blk, wide), F32),
            pltpu.VMEM((n_a, n_b, H, 1, wide), F32),
            pltpu.VMEM((n_a, n_b, H, 1, wide), F32),
            pltpu.VMEM((n_a, HD, wide), F32),
            pltpu.VMEM((n_a, 8, wide), F32),
            pltpu.VMEM((n_a, n_a, 8, wide), F32),
            pltpu.VMEM((n_a, H, blk, HD), BF16),
            pltpu.VMEM((n_a, H, blk, HD), BF16),
            pltpu.VMEM((n_y, H, 2, blk, HD), BF16),
            pltpu.VMEM((n_y, H, 2, blk, HD), BF16),
            pltpu.VMEM((n_y, H, 2, blk, HD), BF16),
            pltpu.VMEM((n_y, H, 2, blk, HD), BF16),
            pltpu.VMEM((H, 2, blk, HD), BF16),
            pltpu.VMEM((H, 2, blk, HD), BF16),
            pltpu.VMEM((H, blk, HD), BF16),
            pltpu.VMEM((H, blk, HD), BF16),
            dma((H, 5)), dma((H, 5)),
            dma((n_a, H)), dma((n_a, H)),
            dma((n_a, H)), dma((n_a, H)),
            dma((n_b, H)), dma((n_b, H)),
            dma((n_b, H)), dma((n_b, H)),
            dma((n_a,)), dma((n_a,)),
            dma((n_a,)), dma((n_a,)),
            dma((n_y, H)), dma((n_y, H)),
            dma((n_y, H)), dma((n_y, H)),
            dma((H,)), dma((H,)),
            dma((H,)), dma((H,)),
            dma((5,)),
        ],
        compiler_params=pltpu.CompilerParams(
            collective_id=0, has_side_effects=True, vmem_limit_bytes=56 * 1024 * 1024
        ),
        name="attention_backward",
    )(block_order, query_rows, key_rows, value_rows, layer_out, grad_out, tile_mask)


def solution(mesh):
    rows = P(("qrow", "kcol"), None)
    keys = P(("kcol", "qrow"), None)
    return jax.shard_map(
        functools.partial(body, mesh.shape["qrow"], mesh.shape["kcol"]),
        mesh=mesh,
        in_specs=(rows, keys, keys, rows, rows, P(), P()),
        out_specs=(rows, keys, keys),
        check_vma=False,
    )
```

time: 190 us -> 49.2 us (0.26)
  waiting for transfers between devices: 88.3 us -> 0 us
  Pallas kernels: 0 us -> 44.9 us
  blocking collectives: 44.7 us -> 0 us
  matrix products: 19.5 us -> 0 us
  between operations: 14.2 us -> 0.65 us
  other arithmetic: 9.67 us -> 0 us
  local copies, waits for them, and re-layouts: 12.5 us -> 3.46 us
    reduce_scatter x3 -> x0, waiting for transfers between devices: 86.9 us -> none  [the longest x1 36.3 us: body(): lax.psum_scatter(value_terms, 'qrow', scatter_dimension=0, tiled=True)]
    pallas_call x0 -> x1, Pallas kernels: none -> 44.9 us  [body(): pl.pallas_call(functools.partial(kernel, n_qrow, n_kcol), out_shape=(out,...]
    all_gather x5 -> x0, blocking collectives: 44.7 us -> none  [the longest x2 15.3 us: merged(): everything = jax.tree.map(lambda part: lax.all_gather(part, axis), x)]
    dot_general x22 -> x0, matrix products: 19.5 us -> none  [the longest x4 5.78 us: tile_grads(): jnp.dot(grad_head, value_head.T, preferred_element_type=jnp.float32)]
    unnamed x47 -> x7, local copies, waits for them, and re-layouts: 12.1 us -> 3.46 us
    concatenate x3 -> x0, other arithmetic: 4.17 us -> none  [the longest x1 1.6 us: tile_grads(): jnp.concatenate(value_list, 1)]
    mul x3 -> x0, other arithmetic: 2.65 us -> none  [the longest x1 1.19 us: body(): grad_out.astype(jnp.float32) * layer_out.astype(jnp.float32)]
    reduce_sum x5 -> x0, other arithmetic: 2.23 us -> none  [the longest x4 1.99 us: body(): totals_list.append(jnp.sum(jnp.exp(scores - largest[:, None]), axis=1))]
  transfers between devices with their start and end apart: 5 -> 0, of which waited for: 3 -> 0; matrix products, arithmetic and copies ran while one was open for 13% -> 0% of each run, Pallas kernels for 0% -> 0%
where the time goes in v1:
time: 49.2 us; the launch traced here: 49 us
  Pallas kernels  44.9 us (91%)
  local copies, waits for them, and re-layouts  3.46 us (7%)
  between operations  0.65 us (1%)
    pallas_call x1, Pallas kernels, body(): pl.pallas_call(functools.partial(kernel, n_qrow, n_kcol), out_shape=(out,...  44.9 us
    unnamed x7, local copies, waits for them, and re-layouts  3.46 us

profile of v1, /device:TPU:0, one launch (start us, length us, event | category | flops | bytes accessed | tf_op | source)
XLA Modules:
  0.0 49.0 jit_solution(8627799115297410992)
XLA Ops:
  0.6 44.9 %attention_backward.1 = (f32[128,512]{1,0:T(8,128)}, f32[128,512]{1,0:T(8,128)}, f32[128,512]{1,0:T(8,128)}) custom-call(s32[32]{0:T(128)} %order_ref.1, bf16[128,512]{1,0:T(8,128)(2,1)} %q_ref.1, bf16[128,512]{1,0:T(8,128)(2,1)} %k_ref.1, bf16[128,512]{1,0:T(8,128)(2,1)} %v_ref.1, bf16[128,512]{1,0:T(8,128)(2,1)} %lo_ref.1, bf16[128,512]{1,0:T(8,128)(2,1)} %go_ref.1, ...), custom_call_target="tpu_custom_call" | custom-call | tf_op jit(solution)/shard_map/attention_backward/pallas_call | solution.py:377
  45.6 0.0 copy-start.1
  45.6 1.7 %copy.13 = f32[128,512]{1,0:T(8,128)} copy(f32[128,512]{1,0:T(8,128)} %get-tuple-element.6) | data formatting | bytes 524288
  47.3 0.0 copy-done.1
  47.3 0.0 copy-start
  47.3 0.7 %copy.14 = f32[128,512]{1,0:T(8,128)} copy(f32[128,512]{1,0:T(8,128)S(1)} %copy-done.1) | data formatting | bytes 524288
  48.0 0.3 copy-done
  48.3 0.7 %copy.15 = f32[128,512]{1,0:T(8,128)} copy(f32[128,512]{1,0:T(8,128)S(1)} %copy-done) | data formatting | bytes 524288
Async XLA Ops:
  45.6 1.7 %copy-start.1 = (f32[128,512]{1,0:T(8,128)S(1)}, f32[128,512]{1,0:T(8,128)}, u32[]{:S(2)}) copy-start(f32[128,512]{1,0:T(8,128)} %get-tuple-element.7) | copy-start | bytes 786436
  47.3 1.0 %copy-start = (f32[128,512]{1,0:T(8,128)S(1)}, f32[128,512]{1,0:T(8,128)}, u32[]{:S(2)}) copy-start(f32[128,512]{1,0:T(8,128)} %get-tuple-element.8) | copy-start | bytes 786436

commit v2 on v1

--- a/solution.py
+++ b/solution.py
@@ -28,7 +28,7 @@
     n_qrow, n_kcol,
     order_ref, q_ref, k_ref, v_ref, lo_ref, go_ref, mask_ref,
     gq_ref, gk_ref, gv_ref,
-    qs, gs, ks, vs, dbuf, p_buf, m_buf, c_buf, gqt,
+    qs, gs, ks, vs, dbuf, p_buf, m_buf, c_buf, gqt, acc,
     st, st_in, sa, ra, sib_out, sib_in, y_out, y_in, zk_out, zk_in, zq_out, zq_in,
     z_send, z_recv, aq_send, aq_recv, ag_send, ag_recv, bk_send, bk_recv, bv_send, bv_recv,
     s_send, s_recv, ga_send, ga_recv, sib_send, sib_recv, y_send, y_recv,
@@ -224,6 +224,15 @@
         e = n_a - d
         return remote(st, st_in.at[e], s_send.at[e], s_recv.at[e], a_dev(d))
 
+    turns = (2, 1, 3, 0)
+
+    def queries(a):
+        delta = jnp.concatenate([gs[a, t, blk : blk + DROWS, :][0:1].astype(F32) for t in range(H)], 1)
+        return qs[a].reshape(wide, HD), gs[a, :, :blk, :].reshape(wide, HD), delta
+
+    def dprobs(s, ga, delta):
+        return dot(vs[:, s].reshape(n_b * blk, HD), ga, NT) - delta
+
     for d in range(1, n_a):
         s_copy(d).start()
     onward(v_set)
@@ -231,6 +240,8 @@
         wait_queries(g_set, a)
     for b in range(1, n_b):
         wait_keys(v_set, b)
+    _, last_g, last_delta = queries(n_a - 1)
+    early = {s: dprobs(s, last_g, last_delta) for s in turns[:2]}
     for d in range(1, n_a):
         s_copy(d).wait_recv()
     for a in range(n_a):
@@ -263,23 +274,24 @@
         return remote(sa.at[d], ra.at[e], ga_send.at[e], ga_recv.at[e], a_dev(d))
 
     part = {}
-
-    def compute(s, is_first):
-        gk = gv = None
-        for a in range(n_a):
-            qa = qs[a].reshape(wide, HD)
-            ga = gs[a, :, :blk, :].reshape(wide, HD)
-            delta = jnp.concatenate([gs[a, t, blk : blk + DROWS, :][0:1].astype(F32) for t in range(H)], 1)
-            dp = dot(vs[:, s].reshape(n_b * blk, HD), ga, NT)
-            pr = (p_buf[a, :, s] * c_buf[a, :, s]).reshape(n_b * blk, wide)
-            ds = (pr * (dp - delta)).astype(BF16)
-            dk = dot(ds, qa, NN)
-            dv = dot(pr.astype(BF16), ga, NN)
-            gk = dk if a == 0 else gk + dk
-            gv = dv if a == 0 else gv + dv
-            term = dot(ks[:, s].reshape(n_b * blk, HD), ds, TN)
-            gqt[a] = term if is_first else gqt[a] + term
-        gk = gk * scale
+    def compute(a, s, early):
+        qa, ga, delta = queries(a)
+        dp = dprobs(s, ga, delta) if early is None else early
+        pr = (p_buf[a, :, s] * c_buf[a, :, s]).reshape(n_b * blk, wide)
+        ds = (pr * dp).astype(BF16)
+        dk = dot(ds, qa, NN)
+        dv = dot(pr.astype(BF16), ga, NN)
+        term = dot(ks[:, s].reshape(n_b * blk, HD), ds, TN)
+        gqt[a] = term if s == turns[0] else gqt[a] + term
+        if a == n_a - 1:
+            acc[s, 0], acc[s, 1] = dk, dv
+            return
+        if a:
+            acc[s, 0] += dk
+            acc[s, 1] += dv
+            return
+        gk = (acc[s, 0] + dk) * scale
+        gv = acc[s, 1] + dv
         for d in range(n_y):
             mine = slice(2 * d * blk, (2 * d + 1) * blk)
             other = slice((2 * d + 1) * blk, (2 * d + 2) * blk)
@@ -309,21 +321,20 @@
             zk_out[s, 1] = total[1].astype(BF16)
             zk_copy(s).start()
         else:
-            gk_ref[:, cols(0)] = total[0]
-            gv_ref[:, cols(0)] = total[1]
-
-    turns = (2, 1, 3, 0)
+            gk_ref[:, cols(0)] = total[0].astype(BF16)
+            gv_ref[:, cols(0)] = total[1].astype(BF16)
+
+    for a in range(n_a - 1, 0, -1):
+        for s in turns:
+            compute(a, s, early.get(s) if a == n_a - 1 else None)
+        sa[a] = (gqt[a].T * scale).astype(BF16).reshape(H, blk, HD)
+        ga_copy(a).start()
     for i, s in enumerate(turns):
-        compute(s, i == 0)
+        compute(0, s, None)
         if i >= 1:
             finish_y(turns[i - 1])
         if i >= 2:
             finish_z(turns[i - 2])
-    for a in range(1, n_a):
-        sa[a] = (gqt[a].T * scale).astype(BF16).reshape(H, blk, HD)
-        ga_copy(a).start()
-    finish_y(turns[3])
-    finish_z(turns[2])
     total_q = (gqt[0].T * scale).reshape(H, blk, HD)
     for d in range(1, n_a):
         ga_copy(n_a - d).wait_recv()
@@ -331,16 +342,18 @@
     for d in (2, 1, 3):
         zq_out[d] = total_q[d].astype(BF16)
         zq_copy(d).start()
-    gq_ref[:, cols(0)] = total_q[0]
+    finish_y(turns[3])
+    finish_z(turns[2])
+    gq_ref[:, cols(0)] = total_q[0].astype(BF16)
     finish_z(turns[3])
 
     for d in (1, 3, 2):
         zk_copy(H - d).wait_recv()
-        gk_ref[:, cols(d)] = zk_in[d, 0].astype(F32)
-        gv_ref[:, cols(d)] = zk_in[d, 1].astype(F32)
+        gk_ref[:, cols(d)] = zk_in[d, 0]
+        gv_ref[:, cols(d)] = zk_in[d, 1]
     for d in (1, 3, 2):
         zq_copy(H - d).wait_recv()
-        gq_ref[:, cols(d)] = zq_in[d].astype(F32)
+        gq_ref[:, cols(d)] = zq_in[d]
 
     for d in range(1, H):
         for i in range(5):
@@ -373,8 +386,8 @@
     vm = pl.BlockSpec(memory_space=pltpu.VMEM)
     sm = pl.BlockSpec(memory_space=pltpu.SMEM)
     dma = pltpu.SemaphoreType.DMA
-    out = jax.ShapeDtypeStruct(query_rows.shape, F32)
-    return pl.pallas_call(
+    out = jax.ShapeDtypeStruct(query_rows.shape, BF16)
+    grads = pl.pallas_call(
         functools.partial(kernel, n_qrow, n_kcol),
         out_shape=(out, out, out),
         in_specs=[sm, vm, vm, vm, vm, vm, vm],
@@ -389,6 +402,7 @@
             pltpu.VMEM((n_a, n_b, H, 1, wide), F32),
             pltpu.VMEM((n_a, n_b, H, 1, wide), F32),
             pltpu.VMEM((n_a, HD, wide), F32),
+            pltpu.VMEM((H, 2, n_b * blk, HD), F32),
             pltpu.VMEM((n_a, 8, wide), F32),
             pltpu.VMEM((n_a, n_a, 8, wide), F32),
             pltpu.VMEM((n_a, H, blk, HD), BF16),
@@ -419,6 +433,7 @@
         ),
         name="attention_backward",
     )(block_order, query_rows, key_rows, value_rows, layer_out, grad_out, tile_mask)
+    return tuple(grad.astype(F32) for grad in grads)
 
 
 def solution(mesh):

time: 49.2 us -> 49.5 us (level)
  local copies, waits for them, and re-layouts: 3.46 us -> 0.23 us
  other arithmetic: 0 us -> 3.13 us
    unnamed x7 -> x4, local copies, waits for them, and re-layouts: 3.46 us -> 0.23 us
    convert_element_type x0 -> x3, other arithmetic: none -> 3.13 us  [body(): return tuple((grad.astype(F32) for grad in grads))]
where the time goes in v2:
time: 49.5 us; the launch traced here: 49.3 us
  Pallas kernels  45.3 us (92%)
  other arithmetic  3.13 us (6%)
  between operations  0.65 us (1%)
    pallas_call x1, Pallas kernels, body(): pl.pallas_call(functools.partial(kernel, n_qrow, n_kcol), out_shape=(out,...  45.3 us
    convert_element_type x3, other arithmetic, body(): return tuple((grad.astype(F32) for grad in grads))  3.13 us

profile of v2, /device:TPU:0, one launch (start us, length us, event | category | flops | bytes accessed | tf_op | source)
XLA Modules:
  0.0 49.3 jit_solution(16442136136623315768)
XLA Ops:
  0.6 45.3 %attention_backward.1 = (bf16[128,512]{1,0:T(8,128)(2,1)}, bf16[128,512]{1,0:T(8,128)(2,1)}, bf16[128,512]{1,0:T(8,128)(2,1)}) custom-call(s32[32]{0:T(128)} %order_ref.1, bf16[128,512]{1,0:T(8,128)(2,1)} %q_ref.1, bf16[128,512]{1,0:T(8,128)(2,1)} %k_ref.1, bf16[128,512]{1,0:T(8,128)(2,1)} %v_ref.1, bf16[128,512]{1,0:T(8,128)(2,1)} %lo_ref.1, ...), custom_call_target="tpu_custom_call" | custom-call | tf_op jit(solution)/shard_map/attention_backward/pallas_call | solution.py:390
  46.0 0.0 copy-start.1
  46.0 1.7 %convert_element_type.9 = f32[128,512]{1,0:T(8,128)} convert(bf16[128,512]{1,0:T(8,128)(2,1)} %get-tuple-element.6) | non-fusion elementwise | flops 65536 | bytes 393216 | tf_op jit(solution)/shard_map/convert_element_type | solution.py:436
  47.6 0.0 copy-done.1
  47.6 0.0 copy-start
  47.6 0.7 %convert_element_type.10 = f32[128,512]{1,0:T(8,128)} convert(bf16[128,512]{1,0:T(8,128)(2,1)S(1)} %copy-done.1) | non-fusion elementwise | flops 65536 | bytes 393216 | tf_op jit(solution)/shard_map/convert_element_type | solution.py:436
  48.4 0.2 copy-done
  48.6 0.7 %convert_element_type.11 = f32[128,512]{1,0:T(8,128)} convert(bf16[128,512]{1,0:T(8,128)(2,1)S(1)} %copy-done) | non-fusion elementwise | flops 65536 | bytes 393216 | tf_op jit(solution)/shard_map/convert_element_type | solution.py:436
Async XLA Ops:
  46.0 1.7 %copy-start.1 = (bf16[128,512]{1,0:T(8,128)(2,1)S(1)}, bf16[128,512]{1,0:T(8,128)(2,1)}, u32[]{:S(2)}) copy-start(bf16[128,512]{1,0:T(8,128)(2,1)} %get-tuple-element.7) | copy-start | bytes 393220
  47.6 1.0 %copy-start = (bf16[128,512]{1,0:T(8,128)(2,1)S(1)}, bf16[128,512]{1,0:T(8,128)(2,1)}, u32[]{:S(2)}) copy-start(bf16[128,512]{1,0:T(8,128)(2,1)} %get-tuple-element.8) | copy-start | bytes 393220

commit v3 on v1

--- a/solution.py
+++ b/solution.py
@@ -224,6 +224,15 @@
         e = n_a - d
         return remote(st, st_in.at[e], s_send.at[e], s_recv.at[e], a_dev(d))
 
+    turns = (2, 1, 3, 0)
+
+    def queries(a):
+        delta = jnp.concatenate([gs[a, t, blk : blk + DROWS, :][0:1].astype(F32) for t in range(H)], 1)
+        return qs[a].reshape(wide, HD), gs[a, :, :blk, :].reshape(wide, HD), delta
+
+    def dprobs(s, ga, delta):
+        return dot(vs[:, s].reshape(n_b * blk, HD), ga, NT) - delta
+
     for d in range(1, n_a):
         s_copy(d).start()
     onward(v_set)
@@ -231,6 +240,7 @@
         wait_queries(g_set, a)
     for b in range(1, n_b):
         wait_keys(v_set, b)
+    early = [dprobs(turns[0], *queries(a)[1:]) for a in range(n_a)]
     for d in range(1, n_a):
         s_copy(d).wait_recv()
     for a in range(n_a):
@@ -264,21 +274,22 @@
 
     part = {}
 
-    def compute(s, is_first):
+    def compute(s, dps, is_last):
         gk = gv = None
-        for a in range(n_a):
-            qa = qs[a].reshape(wide, HD)
-            ga = gs[a, :, :blk, :].reshape(wide, HD)
-            delta = jnp.concatenate([gs[a, t, blk : blk + DROWS, :][0:1].astype(F32) for t in range(H)], 1)
-            dp = dot(vs[:, s].reshape(n_b * blk, HD), ga, NT)
+        for a in range(n_a - 1, -1, -1):
+            qa, ga, delta = queries(a)
+            dp = dps[a] if dps else dprobs(s, ga, delta)
             pr = (p_buf[a, :, s] * c_buf[a, :, s]).reshape(n_b * blk, wide)
-            ds = (pr * (dp - delta)).astype(BF16)
+            ds = (pr * dp).astype(BF16)
+            term = dot(ks[:, s].reshape(n_b * blk, HD), ds, TN)
+            gqt[a] = term if dps else gqt[a] + term
+            if is_last and a:
+                sa[a] = (gqt[a].T * scale).astype(BF16).reshape(H, blk, HD)
+                ga_copy(a).start()
             dk = dot(ds, qa, NN)
             dv = dot(pr.astype(BF16), ga, NN)
-            gk = dk if a == 0 else gk + dk
-            gv = dv if a == 0 else gv + dv
-            term = dot(ks[:, s].reshape(n_b * blk, HD), ds, TN)
-            gqt[a] = term if is_first else gqt[a] + term
+            gk = dk if gk is None else gk + dk
+            gv = dv if gv is None else gv + dv
         gk = gk * scale
         for d in range(n_y):
             mine = slice(2 * d * blk, (2 * d + 1) * blk)
@@ -312,16 +323,12 @@
             gk_ref[:, cols(0)] = total[0]
             gv_ref[:, cols(0)] = total[1]
 
-    turns = (2, 1, 3, 0)
     for i, s in enumerate(turns):
-        compute(s, i == 0)
+        compute(s, early if i == 0 else None, i == H - 1)
         if i >= 1:
             finish_y(turns[i - 1])
         if i >= 2:
             finish_z(turns[i - 2])
-    for a in range(1, n_a):
-        sa[a] = (gqt[a].T * scale).astype(BF16).reshape(H, blk, HD)
-        ga_copy(a).start()
     finish_y(turns[3])
     finish_z(turns[2])
     total_q = (gqt[0].T * scale).reshape(H, blk, HD)
@@ -364,6 +371,17 @@
                 y_sum(d, s).wait_send()
 
 
+def hand_on(gq, gk, gv, gq_out, gk_out, gv_out, sem):
+    copies = [
+        pltpu.make_async_copy(src, dst, sem.at[i])
+        for i, (src, dst) in enumerate([(gq, gq_out), (gk, gk_out), (gv, gv_out)])
+    ]
+    for copy in copies:
+        copy.start()
+    for copy in copies:
+        copy.wait()
+
+
 def body(n_qrow, n_kcol, query_rows, key_rows, value_rows, layer_out, grad_out, block_order, tile_mask):
     blk = query_rows.shape[0]
     n_a = (n_qrow // (2 * H)) * 2
@@ -374,7 +392,7 @@
     sm = pl.BlockSpec(memory_space=pltpu.SMEM)
     dma = pltpu.SemaphoreType.DMA
     out = jax.ShapeDtypeStruct(query_rows.shape, F32)
-    return pl.pallas_call(
+    grads = pl.pallas_call(
         functools.partial(kernel, n_qrow, n_kcol),
         out_shape=(out, out, out),
         in_specs=[sm, vm, vm, vm, vm, vm, vm],
@@ -419,6 +437,15 @@
         ),
         name="attention_backward",
     )(block_order, query_rows, key_rows, value_rows, layer_out, grad_out, tile_mask)
+    anywhere = pl.BlockSpec(memory_space=pl.ANY)
+    return pl.pallas_call(
+        hand_on,
+        out_shape=(out, out, out),
+        in_specs=[anywhere] * 3,
+        out_specs=(anywhere,) * 3,
+        scratch_shapes=[dma((3,))],
+        name="hand_on",
+    )(*grads)
 
 
 def solution(mesh):

time: 49.2 us -> 70.8 us (1.44)
  Pallas kernels: 44.9 us -> 70 us
  local copies, waits for them, and re-layouts: 3.46 us -> 0 us
    pallas_call x0 -> x1, Pallas kernels: none -> 25 us  [body(): pl.pallas_call(hand_on, out_shape=(out, out, out), in_specs=[anywhere] *...]
    unnamed x7 -> x0, local copies, waits for them, and re-layouts: 3.46 us -> none
where the time goes in v3:
time: 70.8 us; the launch traced here: 70.7 us
  Pallas kernels  70 us (99%)
    pallas_call x1, Pallas kernels, body(): pl.pallas_call(functools.partial(kernel, n_qrow, n_kcol), out_shape=(out,...  45.1 us
    pallas_call x1, Pallas kernels, body(): pl.pallas_call(hand_on, out_shape=(out, out, out), in_specs=[anywhere] *...  25 us

profile of v3, /device:TPU:0, one launch (start us, length us, event | category | flops | bytes accessed | tf_op | source)
XLA Modules:
  0.0 70.7 jit_solution(10962399674749325049)
XLA Ops:
  0.6 45.1 %attention_backward.1 = (f32[128,512]{1,0:T(8,128)}, f32[128,512]{1,0:T(8,128)}, f32[128,512]{1,0:T(8,128)}) custom-call(s32[32]{0:T(128)} %order_ref.1, bf16[128,512]{1,0:T(8,128)(2,1)} %q_ref.1, bf16[128,512]{1,0:T(8,128)(2,1)} %k_ref.1, bf16[128,512]{1,0:T(8,128)(2,1)} %v_ref.1, bf16[128,512]{1,0:T(8,128)(2,1)} %lo_ref.1, bf16[128,512]{1,0:T(8,128)(2,1)} %go_ref.1, ...), custom_call_target="tpu_custom_call" | custom-call | tf_op jit(solution)/shard_map/attention_backward/pallas_call | solution.py:395
  45.7 25.0 %hand_on.1 = (f32[128,512]{1,0:T(8,128)}, f32[128,512]{1,0:T(8,128)}, f32[128,512]{1,0:T(8,128)}) custom-call(f32[128,512]{1,0:T(8,128)} %get-tuple-element.6.gq, f32[128,512]{1,0:T(8,128)} %get-tuple-element.7.gk, f32[128,512]{1,0:T(8,128)} %get-tuple-element.8.gv), custom_call_target="tpu_custom_call" | custom-call | tf_op jit(solution)/shard_map/hand_on/pallas_call | solution.py:441
